TPU v7x, 256 devices: a whole 4x4x8 slice. The times are simulated.
256 devices in a mesh: rows: 4 (over y_lo, core), shard: 64 (over x, y_hi, z).
Axes of the slice: x: 4, y: 4 (y_hi: 2, y_lo: 2; y = y_hi * 2 + y_lo), z: 8, core: 2. Of those that a mesh axis runs over, the one named last changes fastest.
Arguments:
- hidden_in: bfloat16 [128, 14336], P('rows', 'shard'), may hold values from -6 to 6
- resid: bfloat16 [128, 3584], P('rows'), may hold values from -6 to 6
- down_one: bfloat16 [14336, 3584], P('shard'), may hold values from -0.046875 to 0.046875
- gain_one: float32 [3584], replicated, may hold values from 0.5 to 1.5
- enc_weight: bfloat16 [3584, 65536], P(None, ('rows', 'shard')), may hold values from -0.09375 to 0.09375
- enc_bias: float32 [65536], P(('rows', 'shard')), may hold values from -3 to 3
- dec_weight: bfloat16 [65536, 3584], P(('rows', 'shard')), may hold values from -0.09375 to 0.09375
- dec_bias: float32 [3584], replicated, may hold values from -3 to 3
- gain_pre: float32 [3584], replicated, may hold values from 0.5 to 1.5
- gate_two: bfloat16 [3584, 14336], P(None, 'shard'), may hold values from -0.09375 to 0.09375
- up_two: bfloat16 [3584, 14336], P(None, 'shard'), may hold values from -0.09375 to 0.09375
- down_two: bfloat16 [14336, 3584], P('shard'), may hold values from -0.046875 to 0.046875
- gain_post: float32 [3584], replicated, may hold values from 0.5 to 1.5
Outputs:
- latents: bfloat16 [128, 65536], P(None, ('rows', 'shard'))
- delta: float32 [128, 3584], P('rows', 'shard')
All inputs are finite; a program needn't handle non-finite values.
Results may differ from a plain program's by a relative error of at most 0.0064.
Values may be sent and summed in bfloat16 or wider, within the bound.
A program may use at most 64 MiB of HBM per device.

v0:
```python
import jax
import jax.numpy as jnp
from jax import lax
from jax.sharding import PartitionSpec as P

D = 3584


def on_device(
    hidden_in,
    resid,
    down_one,
    gain_one,
    enc_weight,
    enc_bias,
    dec_weight,
    dec_bias,
    gain_pre,
    gate_two,
    up_two,
    down_two,
    gain_post,
):
    n_shard = lax.axis_size("shard")
    columns = D // n_shard
    offset = lax.axis_index("shard") * columns
    first_part = jnp.dot(hidden_in, down_one, preferred_element_type=jnp.float32)
    first = lax.psum(first_part, "shard")
    mean_sq = jnp.mean(first * first, axis=1, keepdims=True)
    clean = (resid.astype(jnp.float32) + first * lax.rsqrt(mean_sq + 1e-06) * gain_one).astype(
        jnp.bfloat16
    )
    clean_all = lax.all_gather(clean, "rows", axis=0, tiled=True)
    centered = (clean_all.astype(jnp.float32) - dec_bias).astype(jnp.bfloat16)
    pre_act = jnp.dot(centered, enc_weight, preferred_element_type=jnp.float32) + enc_bias
    latents = jnp.maximum(pre_act, 0.0).astype(jnp.bfloat16)
    group_sums = lax.psum_scatter(
        jnp.dot(latents, dec_weight, preferred_element_type=jnp.float32),
        "rows",
        scatter_dimension=0,
        tiled=True,
    )
    total = lax.psum(group_sums, "shard")
    recon = (total + dec_bias).astype(jnp.bfloat16)
    stream = jnp.concatenate([clean, recon], axis=0)
    upcast = stream.astype(jnp.float32)
    in_sq = jnp.mean(upcast * upcast, axis=1, keepdims=True)
    normed = (upcast * lax.rsqrt(in_sq + 1e-06) * gain_pre).astype(jnp.bfloat16)
    gate_out = jnp.dot(normed, gate_two, preferred_element_type=jnp.float32)
    up_out = jnp.dot(normed, up_two, preferred_element_type=jnp.float32)
    act = (jax.nn.gelu(gate_out, approximate=True) * up_out).astype(jnp.bfloat16)
    second_part = jnp.dot(act, down_two, preferred_element_type=jnp.float32)
    second_cols = lax.psum_scatter(second_part, "shard", scatter_dimension=1, tiled=True)
    second_sq = lax.psum(jnp.sum(second_cols * second_cols, axis=1), "shard")
    stream_cols = lax.dynamic_slice_in_dim(upcast, offset, columns, 1)
    post_cols = lax.dynamic_slice_in_dim(gain_post, offset, columns, 0)
    outputs = stream_cols + second_cols * lax.rsqrt(second_sq[:, None] / D + 1e-06) * post_cols
    half = clean.shape[0]
    delta = outputs[half:] - outputs[:half]
    return (latents, delta)


def solution(mesh):
    in_specs = (
        P("rows", "shard"),
        P("rows", None),
        P("shard", None),
        P(),
        P(None, ("rows", "shard")),
        P(("rows", "shard")),
        P(("rows", "shard"), None),
        P(),
        P(),
        P(None, "shard"),
        P(None, "shard"),
        P("shard", None),
        P(),
    )
    out_specs = (P(None, ("rows", "shard")), P("rows", "shard"))
    return jax.shard_map(
        on_device, mesh=mesh, in_specs=in_specs, out_specs=out_specs, check_vma=False
    )
```

profile of v0, /device:TPU:8, one launch (start us, length us, event | category | flops | bytes accessed | tf_op | source)
XLA Modules:
  0.0 2275.2 jit_solution(13110349626699264122)
XLA Ops:
  7.2 0.0 copy-start
  7.2 0.0 all-reduce.5.cloned.1.call-start
  7.2 2.7 fusion.22
  10.0 0.0 all-reduce.5.cloned.1.call-update
  10.0 0.0 reduce-scatter.3.cloned.1.call-start
  10.1 678.9 %all-reduce.5.cloned.1.call-done = f32[32,3584]{1,0:T(8,128)} async-done(((f32[32,3584]{1,0:T(8,128)}), f32[32,3584]{1,0:T(8,128)}) %all-reduce.5.cloned.1.call-update) | async-done | bytes 458768 | tf_op jit(solution)/shard_map/psum | solution.py:28
  689.0 1.3 multiply_reduce_fusion.1
  690.3 1.2 add_convert_fusion.1
  691.5 8.9 all_gather.3
  700.4 0.4 fusion.1
  700.8 0.0 copy-start.2
  700.9 1.7 fusion.23
  702.5 0.0 reduce-scatter.3.cloned.1.call-update
  702.6 0.0 all-reduce.7.cloned.1.call-start
  702.6 22.3 reduce-scatter.3.cloned.1.call-done
  724.9 0.0 all-reduce.7.cloned.1.call-update
  725.0 0.0 all-reduce.9.cloned.1.call-start
  725.0 680.6 %all-reduce.7.cloned.1.call-done = f32[32,3584]{1,0:T(8,128)} async-done(((f32[32,3584]{1,0:T(8,128)}), f32[32,3584]{1,0:T(8,128)}) %all-reduce.7.cloned.1.call-update) | async-done | bytes 458768 | tf_op jit(solution)/shard_map/psum | solution.py:43
  1405.6 1.0 add_convert_fusion
  1406.7 0.2 multiply_reduce_fusion
  1406.9 2.1 fusion.21
  1408.9 0.0 copy-start.8
  1409.0 4.3 fusion.3
  1413.2 0.0 all-reduce.9.cloned.1.call-update
  1413.3 0.6 dynamic-slice
  1414.5 0.8 dynamic_slice.7
  1415.3 0.1 maximum_convert_fusion
  1415.3 672.4 %all-reduce.9.cloned.1.call-done = f32[64,3584]{1,0:T(8,128)} async-done(((f32[64,3584]{1,0:T(8,128)}), f32[64,3584]{1,0:T(8,128)}) %all-reduce.9.cloned.1.call-update) | async-done | bytes 917520
  2087.8 1.0 multiply_reduce_fusion.2
  2088.8 178.3 %psum.23 = f32[64]{0:T(128)S(1)} all-reduce(f32[64]{0:T(128)S(1)} %multiply_reduce_fusion.2), channel_id=1, replica_groups=mesh['rows'=4,'shard'=64] {'shard'}, use_global_device_ids=true, to_apply=%region_7.0 | all-reduce | flops 64 | bytes 512 | tf_op jit(solution)/shard_map/psum | solution.py:54
  2267.1 0.9 multiply_add_fusion
  2268.0 0.6 slice_subtract_fusion
  (18 shorter events, 0.1 us)
Async XLA Ops:
  7.2 693.7 %copy-start = (bf16[256,3584]{1,0:T(8,128)(2,1)S(1)}, bf16[256,3584]{1,0:T(8,128)(2,1)}, u32[]{:S(2)}) copy-start(bf16[256,3584]{1,0:T(8,128)(2,1)} %param.19) | copy-start | bytes 5505028
  7.2 683.1 %copy-start.1 = (bf16[32,3584]{1,0:T(8,128)(2,1)S(1)}, bf16[32,3584]{1,0:T(8,128)(2,1)}, u32[]{:S(2)}) copy-start(bf16[32,3584]{1,0:T(8,128)(2,1)} %param.14) | copy-start | bytes 688132
  7.2 683.1 %copy-start.3 = (f32[3584]{0:T(1024)S(1)}, f32[3584]{0:T(1024)}, u32[]{:S(2)}) copy-start(f32[3584]{0:T(1024)} %param.16) | copy-start | bytes 43012
  7.2 681.8 %all-reduce.5.cloned.1.call-start = ((), (), s32[]{:S(2)}) async-start(), calls=%async_computation.1 | async-start | bytes 917504 | tf_op jit(solution)/shard_map/psum | solution.py:28
  10.0 690.4 %copy-start.5 = (f32[3584]{0:T(1024)S(1)}, f32[3584]{0:T(1024)}, u32[]{:S(2)}) copy-start(f32[3584]{0:T(1024)} %param.20) | copy-start | bytes 43012
  10.0 690.4 %copy-start.7 = (f32[256]{0:T(256)S(1)}, f32[256]{0:T(256)}, u32[]{:S(2)}) copy-start(f32[256]{0:T(256)} %param.18) | copy-start | bytes 3076
  10.0 714.9 %reduce-scatter.3.cloned.1.call-start = ((), (), s32[]{:S(2)}) async-start(), calls=%async_computation.2 | async-start | bytes 2293760 | tf_op jit(solution)/shard_map/reduce_scatter | solution.py:37
  689.0 11.4 copy-start.6
  700.8 1.7 copy-start.2
  702.5 704.4 %copy-start.4 = (f32[3584]{0:T(1024)S(1)}, f32[3584]{0:T(1024)}, u32[]{:S(2)}) copy-start(f32[3584]{0:T(1024)} %param.21) | copy-start | bytes 43012
  702.6 703.1 %all-reduce.7.cloned.1.call-start = ((), (), s32[]{:S(2)}) async-start(), calls=%async_computation.3 | async-start | bytes 917504 | tf_op jit(solution)/shard_map/psum | solution.py:43
  725.0 1362.8 %all-reduce.9.cloned.1.call-start = ((), (), s32[]{:S(2)}) async-start(), calls=%async_computation.4 | async-start | bytes 1835008
  1408.9 4.3 copy-start.8
Sparse Core Ops, SparseCore 0:
  10.7 678.3 all-reduce.4
  702.7 22.2 reduce-scatter.2
  727.7 677.8 all-reduce.6
  1413.4 674.3 all-reduce.8
where the time goes:
time: 2280 us
  waiting for transfers between devices  2050 us (90%)
  blocking collectives  187 us (8%)
    psum x1, waiting for transfers between devices, on_device(): total = lax.psum(group_sums, 'shard')  681 us
    psum x1, waiting for transfers between devices, on_device(): first = lax.psum(first_part, 'shard')  679 us
    unnamed x5, waiting for transfers between devices  673 us
    psum x1, blocking collectives, on_device(): second_sq = lax.psum(jnp.sum(second_cols * second_cols, axis=1), 'shard')  178 us
  transfers between devices with their start and end apart: 4, of which 4 were waited for; matrix products, arithmetic and copies ran while one was open for 0% of the time, Pallas kernels for 0%

commit v1 on v0

--- a/solution.py
+++ b/solution.py
@@ -40,7 +40,8 @@
         scatter_dimension=0,
         tiled=True,
     )
-    total = lax.psum(group_sums, "shard")
+    pieces = lax.all_gather(group_sums, "shard")
+    total = jnp.sum(pieces, axis=0)
     recon = (total + dec_bias).astype(jnp.bfloat16)
     stream = jnp.concatenate([clean, recon], axis=0)
     upcast = stream.astype(jnp.float32)

time: 2280 us -> 1900 us (0.83)
  waiting for transfers between devices: 2050 us -> 1670 us
    psum x1 -> x0, waiting for transfers between devices: 681 us -> none  [on_device(): total = lax.psum(group_sums, 'shard')]
    all_gather x0 -> x1, waiting for transfers between devices: none -> 296 us  [on_device(): pieces = lax.all_gather(group_sums, 'shard')]
where the time goes in v1:
time: 1900 us
  waiting for transfers between devices  1670 us (88%)
  blocking collectives  187 us (10%)
    psum x1, waiting for transfers between devices, on_device(): first = lax.psum(first_part, 'shard')  679 us
    unnamed x5, waiting for transfers between devices  675 us
    all_gather x1, waiting for transfers between devices, on_device(): pieces = lax.all_gather(group_sums, 'shard')  296 us
    psum x1, blocking collectives, on_device(): second_sq = lax.psum(jnp.sum(second_cols * second_cols, axis=1), 'shard')  178 us
  transfers between devices with their start and end apart: 4, of which 4 were waited for; matrix products, arithmetic and copies ran while one was open for 0% of the time, Pallas kernels for 0%

profile of v1, /device:TPU:8, one launch (start us, length us, event | category | flops | bytes accessed | tf_op | source)
XLA Modules:
  0.0 1903.1 jit_solution(3859037385104535289)
XLA Ops:
  7.2 0.0 copy-start
  7.2 0.0 all-reduce.4.cloned.1.call-start
  7.2 2.7 fusion.22
  10.0 0.0 all-reduce.4.cloned.1.call-update
  10.0 0.0 reduce-scatter.3.cloned.1.call-start
  10.1 678.9 %all-reduce.4.cloned.1.call-done = f32[32,3584]{1,0:T(8,128)} async-done(((f32[32,3584]{1,0:T(8,128)}), f32[32,3584]{1,0:T(8,128)}) %all-reduce.4.cloned.1.call-update) | async-done | bytes 458768 | tf_op jit(solution)/shard_map/psum | solution.py:28
  689.0 1.3 multiply_reduce_fusion.1
  690.3 1.2 add_convert_fusion.1
  691.5 8.9 all_gather.9
  700.4 0.4 fusion.1
  700.8 0.0 copy-start.2
  700.9 1.7 fusion.23
  702.5 0.0 reduce-scatter.3.cloned.1.call-update
  702.6 0.0 all-gather.3.cloned.1.call-start
  702.6 22.3 %reduce-scatter.3.cloned.1.call-done = f32[32,3584]{1,0:T(8,128)} async-done(((f32[128,3584]{1,0:T(8,128)}), f32[32,3584]{1,0:T(8,128)}) %reduce-scatter.3.cloned.1.call-update) | async-done | bytes 458768 | tf_op jit(solution)/shard_map/reduce_scatter | solution.py:37
  724.9 0.0 all-gather.3.cloned.1.call-update
  725.0 0.0 all-reduce.6.cloned.1.call-start
  725.0 296.4 %all-gather.3.cloned.1.call-done = f32[2048,3584]{1,0:T(8,128)} async-done(((f32[32,3584]{1,0:T(8,128)}), f32[2048,3584]{1,0:T(8,128)}) %all-gather.3.cloned.1.call-update) | async-done | bytes 29360144 | tf_op jit(solution)/shard_map/all_gather | solution.py:43
  1021.4 10.7 reduce_sum.37
  1032.2 0.2 multiply_reduce_fusion
  1032.4 2.1 fusion.21
  1034.4 0.0 copy-start.8
  1034.4 4.3 fusion.3
  1038.7 0.0 all-reduce.6.cloned.1.call-update
  1038.7 0.6 dynamic-slice
  1040.0 0.8 dynamic_slice.7
  1040.8 0.1 maximum_convert_fusion
  1040.8 674.9 %all-reduce.6.cloned.1.call-done = f32[64,3584]{1,0:T(8,128)} async-done(((f32[64,3584]{1,0:T(8,128)}), f32[64,3584]{1,0:T(8,128)}) %all-reduce.6.cloned.1.call-update) | async-done | bytes 917520
  1715.7 1.0 multiply_reduce_fusion.2
  1716.8 178.3 %psum.15 = f32[64]{0:T(128)S(1)} all-reduce(f32[64]{0:T(128)S(1)} %multiply_reduce_fusion.2), channel_id=1, replica_groups=mesh['rows'=4,'shard'=64] {'shard'}, use_global_device_ids=true, to_apply=%region_7.0 | all-reduce | flops 64 | bytes 512 | tf_op jit(solution)/shard_map/psum | solution.py:55
  1895.1 0.9 multiply_add_fusion
  1896.0 0.6 slice_subtract_fusion
  (19 shorter events, 0.1 us)
Async XLA Ops:
  7.2 693.7 %copy-start = (bf16[256,3584]{1,0:T(8,128)(2,1)S(1)}, bf16[256,3584]{1,0:T(8,128)(2,1)}, u32[]{:S(2)}) copy-start(bf16[256,3584]{1,0:T(8,128)(2,1)} %param.19) | copy-start | bytes 5505028
  7.2 683.1 %copy-start.1 = (bf16[32,3584]{1,0:T(8,128)(2,1)S(1)}, bf16[32,3584]{1,0:T(8,128)(2,1)}, u32[]{:S(2)}) copy-start(bf16[32,3584]{1,0:T(8,128)(2,1)} %param.14) | copy-start | bytes 688132
  7.2 683.1 %copy-start.3 = (f32[3584]{0:T(1024)S(1)}, f32[3584]{0:T(1024)}, u32[]{:S(2)}) copy-start(f32[3584]{0:T(1024)} %param.16) | copy-start | bytes 43012
  7.2 681.8 %all-reduce.4.cloned.1.call-start = ((), (), s32[]{:S(2)}) async-start(), calls=%async_computation.1 | async-start | bytes 917504 | tf_op jit(solution)/shard_map/psum | solution.py:28
  10.0 690.4 %copy-start.5 = (f32[3584]{0:T(1024)S(1)}, f32[3584]{0:T(1024)}, u32[]{:S(2)}) copy-start(f32[3584]{0:T(1024)} %param.20) | copy-start | bytes 43012
  10.0 690.4 %copy-start.7 = (f32[256]{0:T(256)S(1)}, f32[256]{0:T(256)}, u32[]{:S(2)}) copy-start(f32[256]{0:T(256)} %param.18) | copy-start | bytes 3076
  10.0 714.9 %reduce-scatter.3.cloned.1.call-start = ((), (), s32[]{:S(2)}) async-start(), calls=%async_computation.2 | async-start | bytes 2293760 | tf_op jit(solution)/shard_map/reduce_scatter | solution.py:37
  689.0 11.4 copy-start.6
  700.8 1.7 copy-start.2
  702.6 318.8 %all-gather.3.cloned.1.call-start = ((), (), s32[]{:S(2)}) async-start(), calls=%async_computation.3 | async-start | bytes 29818880 | tf_op jit(solution)/shard_map/all_gather | solution.py:43
  725.0 990.8 %all-reduce.6.cloned.1.call-start = ((), (), s32[]{:S(2)}) async-start(), calls=%async_computation.4 | async-start | bytes 1835008
  1021.4 11.0 copy-start.4
  1034.4 4.3 copy-start.8
Sparse Core Ops, SparseCore 0:
  10.7 678.3 all-reduce.3
  702.7 22.2 reduce-scatter.2
  729.2 292.1 all-gather.2
  1038.8 676.8 all-reduce.5
